TPU v7x, 32 devices: a whole 2x2x4 slice. The times are simulated.
32 devices in a mesh: dp: 2 (over x), depth: 4 (over y, core), height: 4 (over z).
Axes of the slice: x: 2, y: 2, z: 4, core: 2. Of those that a mesh axis runs over, the one named last changes fastest.
Arguments:
- volume: bfloat16 [2, 8, 32, 4096], P('dp', 'depth', 'height'), may hold values from -6 to 6
- feature_grad: bfloat16 [2, 8, 32, 4096], P('dp', 'depth', 'height'), may hold values from -0.125 to 0.125
- master_weights: float32 [2, 110592], P(None, ('dp', 'depth', 'height')), may hold values from -0.15625 to 0.15625
- first_moment: float32 [2, 110592], P(None, ('dp', 'depth', 'height')), may hold values from -3 to 3
- second_moment: float32 [2, 110592], P(None, ('dp', 'depth', 'height')), may hold values from 0.1 to 4
Outputs:
- features: bfloat16 [2, 8, 32, 4096], P('dp', 'depth', 'height')
- new_weights: float32 [2, 110592], P(None, ('dp', 'depth', 'height'))
- new_first: float32 [2, 110592], P(None, ('dp', 'depth', 'height'))
- new_second: float32 [2, 110592], P(None, ('dp', 'depth', 'height'))
All inputs are finite; a program needn't handle non-finite values.
Results may differ from a plain program's by a relative error of at most 0.0095.
The roundings to bfloat16 on the way count: a program that leaves them out, or rounds other values in their place, can miss the bound.
Values may be sent and summed in bfloat16 or wider, within the bound.
A program may use at most 192 MiB of HBM per device.

v0:
```python
import functools

import jax
import jax.numpy as jnp
from jax import lax
from jax.experimental import pallas as pl
from jax.experimental.pallas import tpu as pltpu
from jax.sharding import PartitionSpec as P

C = 64
WIDTH = 64

leak_slope = 0.3
first_decay = 0.9
second_decay = 0.999
learn_rate = 0.001
epsilon = 1e-08
step_count = 10

MESH = pl.DeviceIdType.MESH
BF = jnp.bfloat16
F32 = jnp.float32
SIDES = [(a, b) for a in (-1, 0, 1) for b in (-1, 0, 1) if (a, b) != (0, 0)]


def bit_plan(sizes):
    dp, depth, height = sizes
    plan = []
    for k in range(height.bit_length() - 1):
        plan.append((2, 1 << k))
    for k in range(1, depth.bit_length() - 1):
        plan.append((1, 1 << k))
    for k in range(dp.bit_length() - 1):
        plan.append((0, 1 << k))
    plan.append((1, 1))
    return plan


def place_of(plan):
    index = [lax.axis_index("dp"), lax.axis_index("depth"), lax.axis_index("height")]
    bits, partners = [], []
    for axis, unit in plan:
        bit = lax.rem(index[axis] // unit, 2)
        other = list(index)
        other[axis] = index[axis] + (1 - 2 * bit) * unit
        bits.append(bit)
        partners.append(tuple(other))
    return bits, partners


def greet(partners):
    barrier = pltpu.get_barrier_semaphore()
    for partner in partners:
        pl.semaphore_signal(barrier, inc=1, device_id=partner, device_id_type=MESH)
    pl.semaphore_wait(barrier, len(partners))


def gather_kernel(plan, own_ref, all_ref, send_sem, recv_sem):
    bits, partners = place_of(plan)
    place = sum(bit * (1 << k) for k, bit in enumerate(bits))
    greet(partners)
    all_ref[pl.ds(place, 1)] = own_ref[...].astype(BF)[None]
    for k, partner in enumerate(partners):
        size = 1 << k
        start = (place // size) * size
        copy = pltpu.make_async_remote_copy(
            src_ref=all_ref.at[pl.ds(start, size)],
            dst_ref=all_ref.at[pl.ds(start, size)],
            send_sem=send_sem.at[k],
            recv_sem=recv_sem.at[k],
            device_id=partner,
            device_id_type=MESH,
        )
        copy.start()
        copy.wait()


def scatter_kernel(plan, grads_ref, out_ref, acc, outgoing, incoming, send_sem, recv_sem):
    bits, partners = place_of(plan)
    greet(partners)
    base = 0
    for k in reversed(range(len(plan))):
        size = 1 << k
        source = grads_ref if k == len(plan) - 1 else acc
        give = base + (1 - bits[k]) * size
        keep = base + bits[k] * size
        outgoing[pl.ds(size, size)] = source[pl.ds(give, size)].astype(BF)
        copy = pltpu.make_async_remote_copy(
            src_ref=outgoing.at[pl.ds(size, size)],
            dst_ref=incoming.at[pl.ds(size, size)],
            send_sem=send_sem.at[k],
            recv_sem=recv_sem.at[k],
            device_id=partners[k],
            device_id_type=MESH,
        )
        copy.start()
        copy.wait()
        total = source[pl.ds(keep, size)] + incoming[pl.ds(size, size)].astype(F32)
        if k:
            acc[pl.ds(keep, size)] = total
        else:
            out_ref[...] = total[0]
        base = keep


def span(side, cells, arriving):
    if side == 0:
        return pl.ds(1, cells)
    if side < 0:
        return pl.ds(cells + 1 if arriving else 1, 1)
    return pl.ds(0 if arriving else cells, 1)


def shifted(x, step, w):
    rolled = pltpu.roll(x, step % x.shape[0], 0)
    edge = 0 if step == 1 else WIDTH - 1
    return jnp.where(w == edge, 0.0, rolled)


def layers_kernel(
    depth_n,
    height_n,
    vol_ref,
    fg_ref,
    w1_ref,
    w2_ref,
    wb_ref,
    feat_ref,
    grad_ref,
    vol,
    hid,
    del2,
    wide_v,
    wide_h,
    slope1,
    slots,
    send_sem,
    recv_sem,
):
    cells_d, cells_h = vol_ref.shape[0], vol_ref.shape[1]
    rows = cells_d * cells_h * WIDTH
    me_p, me_d, me_h = lax.axis_index("dp"), lax.axis_index("depth"), lax.axis_index("height")
    own = (pl.ds(1, cells_d), pl.ds(1, cells_h))

    def there(a, b):
        d, h = me_d + a, me_h + b
        return (d >= 0) & (d < depth_n) & (h >= 0) & (h < height_n)

    for buffer in (vol, hid, del2):
        for d in (0, cells_d + 1):
            buffer[d] = jnp.zeros_like(buffer[d])
        for h in (0, cells_h + 1):
            buffer[pl.ds(1, cells_d), h] = jnp.zeros((cells_d, WIDTH, C), BF)
    vol[own] = vol_ref[...]

    barrier = pltpu.get_barrier_semaphore()
    for a, b in SIDES:

        @pl.when(there(a, b))
        def _(a=a, b=b):
            pl.semaphore_signal(
                barrier, inc=1, device_id=(me_p, me_d + a, me_h + b), device_id_type=MESH
            )

    near_d = 1 + jnp.where(me_d > 0, 1, 0) + jnp.where(me_d < depth_n - 1, 1, 0)
    near_h = 1 + jnp.where(me_h > 0, 1, 0) + jnp.where(me_h < height_n - 1, 1, 0)
    pl.semaphore_wait(barrier, near_d * near_h - 1)

    def copy_of(buffer, which, n):
        a, b = SIDES[n]
        return pltpu.make_async_remote_copy(
            src_ref=buffer.at[span(a, cells_d, False), span(b, cells_h, False)],
            dst_ref=buffer.at[span(a, cells_d, True), span(b, cells_h, True)],
            send_sem=send_sem.at[which, n],
            recv_sem=recv_sem.at[which, n],
            device_id=(me_p, me_d + a, me_h + b),
            device_id_type=MESH,
        )

    def send(buffer, which):
        for n, (a, b) in enumerate(SIDES):

            @pl.when(there(a, b))
            def _(n=n):
                copy_of(buffer, which, n).start()

    def arrive(buffer, which):
        for n, (a, b) in enumerate(SIDES):

            @pl.when(there(-a, -b))
            def _(n=n):
                copy_of(buffer, which, n).wait_recv()

    def sent(buffer, which):
        for n, (a, b) in enumerate(SIDES):

            @pl.when(there(a, b))
            def _(n=n):
                copy_of(buffer, which, n).wait_send()

    def widen(buffer, wide):
        for b in range(3):
            wide[:, :, :, pl.ds(b * C, C)] = buffer[:, pl.ds(b, cells_h)]

    w_of = lax.broadcasted_iota(jnp.int32, (rows // cells_d, C), 0) % WIDTH

    def conv(wide, weights_ref, d):
        total = None
        for a in range(3):
            term = jnp.dot(
                wide[d + a].reshape(cells_h * WIDTH, 3 * C),
                weights_ref[a],
                preferred_element_type=F32,
            )
            total = term if total is None else total + term
        return (
            shifted(total[:, 0:C], 1, w_of)
            + total[:, C : 2 * C]
            + shifted(total[:, 2 * C : 3 * C], -1, w_of)
        )

    def tripled(delta):
        wide = delta.reshape(cells_d, cells_h * WIDTH, C)
        for d in range(cells_d):
            slots[pl.ds(d * cells_h * WIDTH, cells_h * WIDTH), pl.ds(0, C)] = shifted(
                wide[d], -1, w_of
            ).astype(BF)
            slots[pl.ds(d * cells_h * WIDTH, cells_h * WIDTH), pl.ds(C, C)] = wide[d].astype(BF)
            slots[pl.ds(d * cells_h * WIDTH, cells_h * WIDTH), pl.ds(2 * C, C)] = shifted(
                wide[d], 1, w_of
            ).astype(BF)

    def grad(wide, layer):
        for a in range(3):
            grad_ref[layer, a] = lax.dot_general(
                wide[a : a + cells_d].reshape(rows, 3 * C),
                slots[...],
                (((0,), (0,)), ((), ())),
                preferred_element_type=F32,
            )

    send(vol, 0)
    arrive(vol, 0)
    widen(vol, wide_v)
    for d in range(cells_d):
        linear = conv(wide_v, w1_ref, d)
        slope = jnp.where(linear > 0, 1.0, leak_slope)
        slope1[d] = slope
        hid[d + 1, pl.ds(1, cells_h)] = (linear * slope).astype(BF).reshape(cells_h, WIDTH, C)
    send(hid, 1)
    arrive(hid, 1)
    widen(hid, wide_h)
    for d in range(cells_d):
        linear = conv(wide_h, w2_ref, d)
        slope = jnp.where(linear > 0, 1.0, leak_slope)
        feat_ref[d] = (linear * slope).astype(BF).reshape(cells_h, WIDTH, C)
        given = fg_ref[d].astype(F32).reshape(cells_h * WIDTH, C)
        del2[d + 1, pl.ds(1, cells_h)] = (given * slope).astype(BF).reshape(cells_h, WIDTH, C)
    send(del2, 2)
    tripled(del2[own].astype(F32).reshape(rows, C))
    grad(wide_h, 1)
    arrive(del2, 2)
    widen(del2, wide_h)
    deltas = [conv(wide_h, wb_ref, d) * slope1[d] for d in range(cells_d)]
    tripled(jnp.concatenate(deltas, 0).astype(BF).astype(F32))
    grad(wide_v, 0)
    for which, buffer in enumerate((vol, hid, del2)):
        sent(buffer, which)


def vmem(count):
    return [pl.BlockSpec(memory_space=pltpu.VMEM)] * count


def body(sizes, volume, feature_grad, master_weights, first_moment, second_moment):
    dp_n, depth_n, height_n = sizes
    devices = dp_n * depth_n * height_n
    plan = bit_plan(sizes)
    steps = len(plan)
    cells_d, cells_h = volume.shape[1], volume.shape[2]
    shard = master_weights.shape[1]
    slot_rows = -(-2 * shard // (16 * 128)) * 16
    pad = slot_rows * 128 - 2 * shard

    slot = jnp.pad(master_weights.reshape(-1), (0, pad)).reshape(slot_rows, 128)
    gathered = pl.pallas_call(
        functools.partial(gather_kernel, plan),
        out_shape=jax.ShapeDtypeStruct((devices, slot_rows, 128), BF),
        in_specs=vmem(1),
        out_specs=vmem(1)[0],
        scratch_shapes=[pltpu.SemaphoreType.DMA((steps,)), pltpu.SemaphoreType.DMA((steps,))],
        compiler_params=pltpu.CompilerParams(
            collective_id=0, has_side_effects=True, vmem_limit_bytes=32 * 2**20
        ),
        name="gather_kernels",
    )(slot)
    gathered = gathered.reshape(2, dp_n, depth_n // 2, height_n, slot_rows * 128)[..., : 2 * shard]
    kernels = (
        gathered.reshape(2, dp_n, depth_n // 2, height_n, 2, shard)
        .transpose(4, 1, 2, 0, 3, 5)
        .reshape(2, 3, 3, 3, C, C)
    )
    forward = kernels.transpose(0, 1, 2, 4, 3, 5).reshape(2, 3, 3 * C, 3 * C)
    back = kernels[1, ::-1, ::-1, ::-1].transpose(0, 1, 4, 2, 3).reshape(3, 3 * C, 3 * C)

    block = (cells_d, cells_h, WIDTH, C)
    padded = (cells_d + 2, cells_h + 2, WIDTH, C)
    wide = (cells_d + 2, cells_h, WIDTH, 3 * C)
    features, grads = pl.pallas_call(
        functools.partial(layers_kernel, depth_n, height_n),
        out_shape=(
            jax.ShapeDtypeStruct(block, BF),
            jax.ShapeDtypeStruct((2, 3, 3 * C, 3 * C), F32),
        ),
        in_specs=vmem(5),
        out_specs=tuple(vmem(2)),
        scratch_shapes=[
            pltpu.VMEM(padded, BF),
            pltpu.VMEM(padded, BF),
            pltpu.VMEM(padded, BF),
            pltpu.VMEM(wide, BF),
            pltpu.VMEM(wide, BF),
            pltpu.VMEM((cells_d, cells_h * WIDTH, C), F32),
            pltpu.VMEM((cells_d * cells_h * WIDTH, 3 * C), BF),
            pltpu.SemaphoreType.DMA((3, 8)),
            pltpu.SemaphoreType.DMA((3, 8)),
        ],
        compiler_params=pltpu.CompilerParams(
            collective_id=1, has_side_effects=True, vmem_limit_bytes=48 * 2**20
        ),
        name="two_layers",
    )(volume.reshape(block), feature_grad.reshape(block), forward[0], forward[1], back)
    features = features.reshape(1, cells_d, cells_h, WIDTH * C)

    parts = (
        grads.reshape(2, 3, 3, C, 3, C)
        .transpose(0, 1, 2, 4, 3, 5)
        .reshape(2, dp_n, depth_n // 2, 2, height_n, shard)
        .transpose(3, 1, 2, 4, 0, 5)
        .reshape(devices, 2 * shard)
    )
    parts = jnp.pad(parts, ((0, 0), (0, pad))).reshape(devices, slot_rows, 128)
    summed = pl.pallas_call(
        functools.partial(scatter_kernel, plan),
        out_shape=jax.ShapeDtypeStruct((slot_rows, 128), F32),
        in_specs=vmem(1),
        out_specs=vmem(1)[0],
        scratch_shapes=[
            pltpu.VMEM((devices, slot_rows, 128), F32),
            pltpu.VMEM((devices, slot_rows, 128), BF),
            pltpu.VMEM((devices, slot_rows, 128), BF),
            pltpu.SemaphoreType.DMA((steps,)),
            pltpu.SemaphoreType.DMA((steps,)),
        ],
        compiler_params=pltpu.CompilerParams(
            collective_id=2, has_side_effects=True, vmem_limit_bytes=32 * 2**20
        ),
        name="scatter_grads",
    )(parts)
    summed = summed.reshape(-1)[: 2 * shard].reshape(2, shard)

    new_first = first_decay * first_moment + (1.0 - first_decay) * summed
    new_second = second_decay * second_moment + (1.0 - second_decay) * summed * summed
    first_fix = 1.0 - first_decay**step_count
    second_fix = 1.0 - second_decay**step_count
    new_weights = master_weights - learn_rate * (new_first / first_fix) / (
        jnp.sqrt(new_second / second_fix) + epsilon
    )
    return (features, new_weights, new_first, new_second)


def solution(mesh):
    sizes = (mesh.shape["dp"], mesh.shape["depth"], mesh.shape["height"])
    owners = P(None, ("dp", "depth", "height"))
    blocks = P("dp", "depth", "height", None)
    return jax.shard_map(
        functools.partial(body, sizes),
        mesh=mesh,
        in_specs=(blocks, blocks, owners, owners, owners),
        out_specs=(blocks, owners, owners, owners),
        check_vma=False,
    )
```

profile of v0, /device:TPU:0, one launch (start us, length us, event | category | flops | bytes accessed | tf_op | source)
XLA Modules:
  0.0 69.7 jit_solution(15683672144006623702)
XLA Ops:
  0.6 0.8 %reshape.61 = f32[6912]{0:T(1024)S(1)} reshape(f32[2,3456]{1,0:T(2,128)} %param.7) | data formatting | bytes 55296 | tf_op jit(solution)/shard_map/reshape | solution.py:285
  1.4 1.2 %reshape.59.vol_ref = bf16[2,8,64,64]{3,2,1,0:T(8,128)(2,1)S(1)} reshape(bf16[1,2,8,4096]{3,2,1,0:T(8,128)(2,1)} %param.5) | data formatting | bytes 262144 | tf_op jit(solution)/shard_map/reshape | solution.py:332
  2.6 1.2 %reshape.60.fg_ref = bf16[2,8,64,64]{3,2,1,0:T(8,128)(2,1)S(1)} reshape(bf16[1,2,8,4096]{3,2,1,0:T(8,128)(2,1)} %param.6) | data formatting | bytes 262144 | tf_op jit(solution)/shard_map/reshape | solution.py:332
  3.8 19.3 %gather_kernels.1 = bf16[32,64,128]{2,1,0:T(8,128)(2,1)S(1)} custom-call(f32[64,128]{1,0:T(8,128)S(1)} %pad_bitcast_fusion.1.own_ref), custom_call_target="tpu_custom_call" | custom-call | tf_op jit(solution)/shard_map/gather_kernels/pallas_call | solution.py:286
  23.1 0.1 reshape.63
  23.2 0.2 slice.27
  23.4 0.2 reshape.64
  23.5 0.5 slice.30
  24.0 0.1 copy.16
  24.1 0.2 copy.13
  24.3 0.3 slice.25
  24.6 1.0 %copy.17 = bf16[3,3,64,3,64]{4,3,2,1,0:T(4,128)(2,1)S(1)} copy(bf16[3,3,64,3,64]{2,4,3,1,0:T(8,128)(2,1)S(1)} %reverse_bitcast_fusion) | data formatting | bytes 442368 | tf_op jit(solution)/shard_map/transpose | solution.py:304
  25.6 0.4 reshape.66.wb_ref
  26.0 0.5 reshape.65
  26.5 0.1 fusion.2
  26.6 0.4 copy.15
  27.0 0.4 squeeze.10.w2_ref
  27.3 0.4 copy.14
  27.7 0.4 squeeze.9.w1_ref
  28.1 15.9 %two_layers.1 = (bf16[2,8,64,64]{3,2,1,0:T(8,128)(2,1)S(1)}, f32[2,3,192,192]{3,2,1,0:T(8,128)S(1)}) custom-call(bf16[2,8,64,64]{3,2,1,0:T(8,128)(2,1)S(1)} %reshape.59.vol_ref, bf16[2,8,64,64]{3,2,1,0:T(8,128)(2,1)S(1)} %reshape.60.fg_ref, bf16[3,192,192]{2,1,0:T(8,128)(2,1)S(1)} %squeeze.9.w1_ref, bf16[3,192,192]{2,1,0:T(8,128)(2,1)S(1)} %squeeze.10.w2_ref, ...), custom_call_target="tpu_custom_call" | custom-call | tf_op jit(solution)/shard_map/two_layers/pallas_call | solution.py:309
  44.0 0.9 %reshape.67 = bf16[1,2,8,4096]{3,2,1,0:T(8,128)(2,1)} reshape(bf16[2,8,64,64]{3,2,1,0:T(8,128)(2,1)S(1)} %get-tuple-element.6) | data formatting | bytes 262144 | tf_op jit(solution)/shard_map/reshape | solution.py:333
  44.9 0.7 %reshape.68 = f32[2,3,3,64,3,64]{5,4,3,2,1,0:T(4,128)S(1)} reshape(f32[2,3,192,192]{3,2,1,0:T(8,128)S(1)} %get-tuple-element.7) | data formatting | bytes 1769472 | tf_op jit(solution)/shard_map/reshape | solution.py:336
  45.7 1.5 %copy.18 = f32[2,3,3,3,64,64]{5,4,3,2,1,0:T(8,128)} copy(f32[2,3,3,3,64,64]{5,3,4,2,1,0:T(4,128)S(1)} %bitcast.27) | data formatting | bytes 1769472 | tf_op jit(solution)/shard_map/transpose | solution.py:337
  47.1 2.0 %reshape.69 = f32[2,2,2,2,4,3456]{5,4,3,2,1,0:T(4,128)S(1)} reshape(f32[2,3,3,3,64,64]{5,4,3,2,1,0:T(8,128)} %copy.18) | data formatting | bytes 1769472 | tf_op jit(solution)/shard_map/reshape | solution.py:338
  49.2 0.7 copy.19
  49.9 0.1 copy.20
  49.9 0.1 pad_bitcast_fusion
  50.0 0.0 copy-start
  50.0 0.0 copy-start.1
  50.0 0.0 copy-start.2
  50.1 0.2 copy.21
  50.3 18.6 %scatter_grads.1 = f32[64,128]{1,0:T(8,128)S(1)} custom-call(f32[32,64,128]{2,1,0:T(8,128)S(1)} %bitcast.26), custom_call_target="tpu_custom_call" | custom-call | tf_op jit(solution)/shard_map/scatter_grads/pallas_call | solution.py:343
  68.9 0.0 copy-done
  68.9 0.0 copy-done.1
  68.9 0.0 copy-done.2
  68.9 0.7 %divide_subtract_fusion = (f32[2,3456]{1,0:T(2,128)}, f32[2,3456]{1,0:T(2,128)}, f32[2,3456]{1,0:T(2,128)}) fusion(f32[2,3456]{1,0:T(2,128)S(1)} %copy-done, f32[2,3456]{1,0:T(2,128)S(1)} %reshape.72, f32[2,3456]{1,0:T(2,128)S(1)} %copy-done.1, f32[2,3456]{1,0:T(2,128)S(1)} %copy-done.2), kind=kLoop, calls=%fused_computation.5 | loop fusion | flops 82944 | bytes 193536 | tf_op jit(solution)/shard_map/sub | solution.py:366
  (4 shorter events, 0.1 us)
Async XLA Ops:
  50.0 18.9 %copy-start = (f32[2,3456]{1,0:T(2,128)S(1)}, f32[2,3456]{1,0:T(2,128)}, u32[]{:S(2)}) copy-start(f32[2,3456]{1,0:T(2,128)} %param.7) | copy-start | bytes 82948
  50.0 18.9 %copy-start.1 = (f32[2,3456]{1,0:T(2,128)S(1)}, f32[2,3456]{1,0:T(2,128)}, u32[]{:S(2)}) copy-start(f32[2,3456]{1,0:T(2,128)} %param.8) | copy-start | bytes 82948
  50.0 18.9 %copy-start.2 = (f32[2,3456]{1,0:T(2,128)S(1)}, f32[2,3456]{1,0:T(2,128)}, u32[]{:S(2)}) copy-start(f32[2,3456]{1,0:T(2,128)} %param.9) | copy-start | bytes 82948
where the time goes:
time: 69.9 us; the launch traced here: 69.7 us
  Pallas kernels  53.8 us (77%)
  local copies, waits for them, and re-layouts  14.3 us (20%)
  between operations  0.88 us (1%)
  other arithmetic  0.71 us (1%)
    pallas_call x1, Pallas kernels, body(): pl.pallas_call(functools.partial(gather_kernel, plan), out_shape=jax.Shap...  19.3 us
    pallas_call x1, Pallas kernels, body(): pl.pallas_call(functools.partial(scatter_kernel, plan), out_shape=jax.Sha...  18.6 us
    pallas_call x1, Pallas kernels, body(): pl.pallas_call(functools.partial(layers_kernel, depth_n, height_n), out_s...  15.9 us
    transpose x2, local copies, waits for them, and re-layouts, body(): parts = grads.reshape(2, 3, 3, C, 3, C).transpose(0, 1, 2, 4, 3, 5).resha...  2.17 us
    reshape x1, local copies, waits for them, and re-layouts, body(): parts = grads.reshape(2, 3, 3, C, 3, C).transpose(0, 1, 2, 4, 3, 5).resha...  2.04 us

commit v1 on v0

v1 whole, which is shorter than its diff:
```python
import functools

import jax
import jax.numpy as jnp
from jax import lax
from jax.experimental import pallas as pl
from jax.experimental.pallas import tpu as pltpu
from jax.sharding import PartitionSpec as P

C = 64
WIDTH = 64

leak_slope = 0.3
first_decay = 0.9
second_decay = 0.999
learn_rate = 0.001
epsilon = 1e-08
step_count = 10

MESH = pl.DeviceIdType.MESH
BF = jnp.bfloat16
F32 = jnp.float32
SIDES = [(a, b) for a in (-1, 0, 1) for b in (-1, 0, 1) if (a, b) != (0, 0)]


def bit_plan(sizes):
    dp, depth, height = sizes
    plan = []
    for k in range(height.bit_length() - 1):
        plan.append((2, 1 << k))
    for k in range(1, depth.bit_length() - 1):
        plan.append((1, 1 << k))
    for k in range(dp.bit_length() - 1):
        plan.append((0, 1 << k))
    plan.append((1, 1))
    return plan


def place_of(plan):
    index = [lax.axis_index("dp"), lax.axis_index("depth"), lax.axis_index("height")]
    bits, partners = [], []
    for axis, unit in plan:
        bit = lax.rem(index[axis] // unit, 2)
        other = list(index)
        other[axis] = index[axis] + (1 - 2 * bit) * unit
        bits.append(bit)
        partners.append(tuple(other))
    return bits, partners


def greet(partners):
    barrier = pltpu.get_barrier_semaphore()
    for partner in partners:
        pl.semaphore_signal(barrier, inc=1, device_id=partner, device_id_type=MESH)
    pl.semaphore_wait(barrier, len(partners))


def gather_kernel(
    plan, depth_n, height_n, own_ref, vol_ref, all_ref, wide_ref, vol, send_sem, recv_sem, side_send, side_recv
):
    bits, partners = place_of(plan)
    place = sum(bit * (1 << k) for k, bit in enumerate(bits))
    there, count, id_of = neighbours(depth_n, height_n)
    clear_edges(vol)
    vol[pl.ds(1, vol_ref.shape[0]), pl.ds(1, vol_ref.shape[1])] = vol_ref[...]
    all_ref[pl.ds(place, 1)] = own_ref[...].astype(BF)[None]
    barrier = signal_neighbours(there, id_of)
    for partner in partners:
        pl.semaphore_signal(barrier, inc=1, device_id=partner, device_id_type=MESH)
    pl.semaphore_wait(barrier, count + len(partners))
    halo = Halo(vol, there, id_of, side_send, side_recv)
    for k, partner in enumerate(partners):
        size = 1 << k
        start = (place // size) * size
        copy = pltpu.make_async_remote_copy(
            src_ref=all_ref.at[pl.ds(start, size)],
            dst_ref=all_ref.at[pl.ds(start, size)],
            send_sem=send_sem.at[k],
            recv_sem=recv_sem.at[k],
            device_id=partner,
            device_id_type=MESH,
        )
        copy.start()
        if k == 0:
            halo.send()
        if k == len(partners) - 1:
            halo.arrive()
            widen(vol, wide_ref)
        copy.wait()
    halo.sent()


def scatter_kernel(plan, grads_ref, out_ref, acc, outgoing, incoming, send_sem, recv_sem):
    bits, partners = place_of(plan)
    greet(partners)
    base = 0
    for k in reversed(range(len(plan))):
        size = 1 << k
        source = grads_ref if k == len(plan) - 1 else acc
        give = base + (1 - bits[k]) * size
        keep = base + bits[k] * size
        outgoing[pl.ds(size, size)] = source[pl.ds(give, size)].astype(BF)
        copy = pltpu.make_async_remote_copy(
            src_ref=outgoing.at[pl.ds(size, size)],
            dst_ref=incoming.at[pl.ds(size, size)],
            send_sem=send_sem.at[k],
            recv_sem=recv_sem.at[k],
            device_id=partners[k],
            device_id_type=MESH,
        )
        copy.start()
        copy.wait()
        total = source[pl.ds(keep, size)] + incoming[pl.ds(size, size)].astype(F32)
        if k:
            acc[pl.ds(keep, size)] = total
        else:
            out_ref[...] = total[0]
        base = keep


def span(side, cells, arriving):
    if side == 0:
        return pl.ds(1, cells)
    if side < 0:
        return pl.ds(cells + 1 if arriving else 1, 1)
    return pl.ds(0 if arriving else cells, 1)


def shifted(x, step, w):
    rolled = pltpu.roll(x, step % x.shape[0], 0)
    edge = 0 if step == 1 else WIDTH - 1
    return jnp.where(w == edge, 0.0, rolled)


def neighbours(depth_n, height_n):
    me_p, me_d, me_h = lax.axis_index("dp"), lax.axis_index("depth"), lax.axis_index("height")

    def there(a, b):
        d, h = me_d + a, me_h + b
        return (d >= 0) & (d < depth_n) & (h >= 0) & (h < height_n)

    near_d = 1 + jnp.where(me_d > 0, 1, 0) + jnp.where(me_d < depth_n - 1, 1, 0)
    near_h = 1 + jnp.where(me_h > 0, 1, 0) + jnp.where(me_h < height_n - 1, 1, 0)
    return there, near_d * near_h - 1, lambda a, b: (me_p, me_d + a, me_h + b)


def signal_neighbours(there, id_of):
    barrier = pltpu.get_barrier_semaphore()
    for a, b in SIDES:

        @pl.when(there(a, b))
        def _(a=a, b=b):
            pl.semaphore_signal(barrier, inc=1, device_id=id_of(a, b), device_id_type=MESH)

    return barrier


def clear_edges(buffer):
    depth, height = buffer.shape[0], buffer.shape[1]
    for d in (0, depth - 1):
        buffer[d] = jnp.zeros_like(buffer[d])
    for h in (0, height - 1):
        buffer[pl.ds(1, depth - 2), h] = jnp.zeros((depth - 2, WIDTH, C), BF)


class Halo:
    def __init__(self, buffer, there, id_of, send_sem, recv_sem):
        self.there, self.copies = there, []
        depth, height = buffer.shape[0] - 2, buffer.shape[1] - 2
        for n, (a, b) in enumerate(SIDES):

            def make(n=n, a=a, b=b):
                return pltpu.make_async_remote_copy(
                    src_ref=buffer.at[span(a, depth, False), span(b, height, False)],
                    dst_ref=buffer.at[span(a, depth, True), span(b, height, True)],
                    send_sem=send_sem.at[n],
                    recv_sem=recv_sem.at[n],
                    device_id=id_of(a, b),
                    device_id_type=MESH,
                )

            self.copies.append(make)

    def each(self, sign, act):
        for make, (a, b) in zip(self.copies, SIDES):

            @pl.when(self.there(sign * a, sign * b))
            def _(make=make):
                act(make())

    def send(self):
        self.each(1, lambda copy: copy.start())

    def arrive(self):
        self.each(-1, lambda copy: copy.wait_recv())

    def sent(self):
        self.each(1, lambda copy: copy.wait_send())


def widen(buffer, wide):
    for b in range(3):
        wide[:, :, :, pl.ds(b * C, C)] = buffer[:, pl.ds(b, wide.shape[1])]


def layers_kernel(
    depth_n,
    height_n,
    wide_v,
    fg_ref,
    kern_ref,
    feat_ref,
    grad_ref,
    hid,
    del2,
    wide_h,
    slope1,
    slots,
    weights,
    mixed,
    send_sem,
    recv_sem,
):
    cells_d, cells_h = fg_ref.shape[0], fg_ref.shape[1]
    line = cells_h * WIDTH
    there, count, id_of = neighbours(depth_n, height_n)
    clear_edges(hid)
    clear_edges(del2)
    barrier = signal_neighbours(there, id_of)

    half = C // 2
    for layer in range(2):
        for a in range(3):
            for b in range(3):
                taps = [
                    kern_ref[layer, pl.ds((9 * a + 3 * b + c) * half, half)].astype(F32)
                    for c in range(3)
                ]
                for odd in range(2):
                    at = pl.ds(b * C + odd, half, stride=2)
                    parts = [tap[:, odd * C : (odd + 1) * C] for tap in taps]
                    mixed[a, 0, at, :] = jnp.concatenate(parts[:2], 1)
                    mixed[a, 1, at, :] = jnp.concatenate([parts[2], parts[2]], 1)
            weights[layer, a, :, 0 : 2 * C] = mixed[a, 0].astype(BF)
            weights[layer, a, :, 2 * C : 3 * C] = mixed[a, 1, :, 0:C].astype(BF)

    pl.semaphore_wait(barrier, count)
    hid_halo = Halo(hid, there, id_of, send_sem.at[0], recv_sem.at[0])
    del_halo = Halo(del2, there, id_of, send_sem.at[1], recv_sem.at[1])

    def width_of(rows):
        return lax.broadcasted_iota(jnp.int32, (rows, C), 0) % WIDTH

    def conv(wide, layer, d):
        total = None
        for a in range(3):
            term = jnp.dot(
                wide[d + a].reshape(line, 3 * C), weights[layer, a], preferred_element_type=F32
            )
            total = term if total is None else total + term
        w = width_of(line)
        return (
            shifted(total[:, 0:C], 1, w)
            + total[:, C : 2 * C]
            + shifted(total[:, 2 * C : 3 * C], -1, w)
        )

    def triple(d, first, layers, delta):
        rows = layers * WIDTH
        w = width_of(rows)
        delta = delta.astype(F32).reshape(rows, C)
        at = pl.ds(first * WIDTH, rows)
        slots[d, at, pl.ds(0, C)] = shifted(delta, -1, w).astype(BF)
        slots[d, at, pl.ds(C, C)] = delta.astype(BF)
        slots[d, at, pl.ds(2 * C, C)] = shifted(delta, 1, w).astype(BF)

    def grad(wide, layer):
        tripled = slots[pl.ds(1, cells_d), pl.ds(WIDTH, line)].reshape(cells_d * line, 3 * C)
        for a in range(3):
            result = lax.dot_general(
                wide[a : a + cells_d].reshape(cells_d * line, 3 * C),
                tripled,
                (((0,), (0,)), ((), ())),
                preferred_element_type=F32,
            )
            mixed[a, 0] = result[:, 0 : 2 * C]
            mixed[a, 1, :, 0:C] = result[:, 2 * C : 3 * C]
            even, odd = (
                [mixed[a, n, pl.ds(first, 3 * half, stride=2), :] for n in range(2)]
                for first in range(2)
            )
            for b in range(3):
                for c in range(3):
                    part = (slice(b * half, (b + 1) * half), slice(c % 2 * C, (c % 2 + 1) * C))
                    grad_ref[layer, pl.ds((9 * a + 3 * b + c) * half, half)] = jnp.concatenate(
                        [even[c // 2][part], odd[c // 2][part]], 1
                    )

    for d in range(cells_d):
        linear = conv(wide_v, 0, d)
        slope = jnp.where(linear > 0, 1.0, leak_slope)
        slope1[d] = slope
        hid[d + 1, pl.ds(1, cells_h)] = (linear * slope).astype(BF).reshape(cells_h, WIDTH, C)
    hid_halo.send()
    hid_halo.arrive()
    widen(hid, wide_h)
    for d in range(cells_d):
        linear = conv(wide_h, 1, d)
        slope = jnp.where(linear > 0, 1.0, leak_slope)
        feat_ref[d] = (linear * slope).astype(BF).reshape(cells_h, WIDTH, C)
        given = fg_ref[d].astype(F32).reshape(line, C)
        del2[d + 1, pl.ds(1, cells_h)] = (given * slope).astype(BF).reshape(cells_h, WIDTH, C)
    del_halo.send()
    for d in range(1, cells_d + 1):
        triple(d, 1, cells_h, del2[d, pl.ds(1, cells_h)])
    grad(wide_h, 1)
    del_halo.arrive()
    for d in range(cells_d + 2):
        if d in (0, cells_d + 1):
            triple(d, 0, cells_h + 2, del2[d])
        else:
            triple(d, 0, 1, del2[d, 0])
            triple(d, cells_h + 1, 1, del2[d, cells_h + 1])
    deltas = []
    for d in range(cells_d):
        total = None
        for a in range(3):
            spread = lax.dot_general(
                slots[d + 2 - a],
                weights[1, a],
                (((1,), (1,)), ((), ())),
                preferred_element_type=F32,
            )
            for b in range(3):
                term = spread[(2 - b) * WIDTH : (2 - b) * WIDTH + line, b * C : (b + 1) * C]
                total = term if total is None else total + term
        deltas.append((total * slope1[d]).astype(BF))
    for d in range(cells_d):
        triple(d + 1, 1, cells_h, deltas[d])
    grad(wide_v, 0)
    hid_halo.sent()
    del_halo.sent()


def vmem(count):
    return [pl.BlockSpec(memory_space=pltpu.VMEM)] * count


def body(sizes, volume, feature_grad, master_weights, first_moment, second_moment):
    dp_n, depth_n, height_n = sizes
    devices = dp_n * depth_n * height_n
    plan = bit_plan(sizes)
    steps = len(plan)
    cells_d, cells_h = volume.shape[1], volume.shape[2]
    shard = master_weights.shape[1]
    slot_rows = -(-2 * shard // (16 * 128)) * 16
    pad = slot_rows * 128 - 2 * shard

    slot = jnp.pad(master_weights.reshape(-1), (0, pad)).reshape(slot_rows, 128)
    block = (cells_d, cells_h, WIDTH, C)
    padded = (cells_d + 2, cells_h + 2, WIDTH, C)
    wide = (cells_d + 2, cells_h, WIDTH, 3 * C)
    gathered, wide_volume = pl.pallas_call(
        functools.partial(gather_kernel, plan, depth_n, height_n),
        out_shape=(
            jax.ShapeDtypeStruct((devices, slot_rows, 128), BF),
            jax.ShapeDtypeStruct(wide, BF),
        ),
        in_specs=vmem(2),
        out_specs=tuple(vmem(2)),
        scratch_shapes=[
            pltpu.VMEM(padded, BF),
            pltpu.SemaphoreType.DMA((steps,)),
            pltpu.SemaphoreType.DMA((steps,)),
            pltpu.SemaphoreType.DMA((8,)),
            pltpu.SemaphoreType.DMA((8,)),
        ],
        compiler_params=pltpu.CompilerParams(
            collective_id=0, has_side_effects=True, vmem_limit_bytes=32 * 2**20
        ),
        name="gather_kernels",
    )(slot, volume.reshape(block))
    if shard % 128 == 0:
        unit = (shard // 128, 128)
        gathered = gathered[:, : 2 * shard // 128]
    else:
        unit = (shard,)
        gathered = gathered.reshape(devices, slot_rows * 128)[:, : 2 * shard]
    order = (4, 1, 2, 0, 3) + tuple(range(5, 5 + len(unit)))
    kernels = (
        gathered.reshape((2, dp_n, depth_n // 2, height_n, 2) + unit)
        .transpose(order)
        .reshape(2, devices * shard // 128, 128)
    )

    features, grads = pl.pallas_call(
        functools.partial(layers_kernel, depth_n, height_n),
        out_shape=(
            jax.ShapeDtypeStruct(block, BF),
            jax.ShapeDtypeStruct(kernels.shape, F32),
        ),
        in_specs=vmem(3),
        out_specs=tuple(vmem(2)),
        scratch_shapes=[
            pltpu.VMEM(padded, BF),
            pltpu.VMEM(padded, BF),
            pltpu.VMEM(wide, BF),
            pltpu.VMEM((cells_d, cells_h * WIDTH, C), F32),
            pltpu.VMEM((cells_d + 2, (cells_h + 2) * WIDTH, 3 * C), BF),
            pltpu.VMEM((2, 3, 3 * C, 3 * C), BF),
            pltpu.VMEM((3, 2, 3 * C, 2 * C), F32),
            pltpu.SemaphoreType.DMA((2, 8)),
            pltpu.SemaphoreType.DMA((2, 8)),
        ],
        compiler_params=pltpu.CompilerParams(
            collective_id=1, has_side_effects=True, vmem_limit_bytes=48 * 2**20
        ),
        name="two_layers",
    )(wide_volume, feature_grad.reshape(block), kernels)
    features = features.reshape(1, cells_d, cells_h, WIDTH * C)

    order = (3, 1, 2, 4, 0) + tuple(range(5, 5 + len(unit)))
    parts = grads.reshape((2, dp_n, depth_n // 2, 2, height_n) + unit).transpose(order)
    if len(unit) == 2:
        parts = parts.reshape(devices, 2 * unit[0], 128)
        parts = jnp.pad(parts, ((0, 0), (0, slot_rows - 2 * unit[0]), (0, 0)))
    else:
        parts = jnp.pad(parts.reshape(devices, 2 * shard), ((0, 0), (0, pad)))
        parts = parts.reshape(devices, slot_rows, 128)
    summed = pl.pallas_call(
        functools.partial(scatter_kernel, plan),
        out_shape=jax.ShapeDtypeStruct((slot_rows, 128), F32),
        in_specs=vmem(1),
        out_specs=vmem(1)[0],
        scratch_shapes=[
            pltpu.VMEM((devices, slot_rows, 128), F32),
            pltpu.VMEM((devices, slot_rows, 128), BF),
            pltpu.VMEM((devices, slot_rows, 128), BF),
            pltpu.SemaphoreType.DMA((steps,)),
            pltpu.SemaphoreType.DMA((steps,)),
        ],
        compiler_params=pltpu.CompilerParams(
            collective_id=2, has_side_effects=True, vmem_limit_bytes=32 * 2**20
        ),
        name="scatter_grads",
    )(parts)
    summed = summed.reshape(-1)[: 2 * shard].reshape(2, shard)

    new_first = first_decay * first_moment + (1.0 - first_decay) * summed
    new_second = second_decay * second_moment + (1.0 - second_decay) * summed * summed
    first_fix = 1.0 - first_decay**step_count
    second_fix = 1.0 - second_decay**step_count
    new_weights = master_weights - learn_rate * (new_first / first_fix) / (
        jnp.sqrt(new_second / second_fix) + epsilon
    )
    return (features, new_weights, new_first, new_second)


def solution(mesh):
    sizes = (mesh.shape["dp"], mesh.shape["depth"], mesh.shape["height"])
    owners = P(None, ("dp", "depth", "height"))
    blocks = P("dp", "depth", "height", None)
    return jax.shard_map(
        functools.partial(body, sizes),
        mesh=mesh,
        in_specs=(blocks, blocks, owners, owners, owners),
        out_specs=(blocks, owners, owners, owners),
        check_vma=False,
    )
```

time: 69.9 us -> 58.3 us (0.83)
  local copies, waits for them, and re-layouts: 14.3 us -> 5.97 us
  Pallas kernels: 53.8 us -> 50.6 us
    pallas_call x1, Pallas kernels: 15.9 us -> 12.2 us  [body(): pl.pallas_call(functools.partial(layers_kernel, depth_n, height_n), out_s...]
    reshape x6 -> x2, local copies, waits for them, and re-layouts: 3.98 us -> 0.58 us  [the longest x1 0.52 us: body(): parts = parts.reshape(devices, 2 * unit[0], 128)]
    transpose x5 -> x2, local copies, waits for them, and re-layouts: 3.34 us -> 0.57 us  [the longest x1 0.34 us: body(): kernels = gathered.reshape((2, dp_n, depth_n // 2, height_n, 2) + unit).t...]
    slice x7 -> x2, local copies, waits for them, and re-layouts: 1.85 us -> 0.1 us  [body(): gathered = gathered[:, :2 * shard // 128]]
    reshape x1, local copies, waits for them, and re-layouts: 1.18 us -> 0.24 us  [body(): feature_grad.reshape(block)]
    squeeze x2 -> x0, local copies, waits for them, and re-layouts: 0.7 us -> none  [the longest x1 0.35 us: body(): forward[1]]
where the time goes in v1:
time: 58.3 us; the launch traced here: 58 us
  Pallas kernels  50.6 us (87%)
  local copies, waits for them, and re-layouts  5.97 us (10%)
  between operations  0.79 us (1%)
  other arithmetic  0.71 us (1%)
    pallas_call x1, Pallas kernels, body(): pl.pallas_call(functools.partial(gather_kernel, plan, depth_n, height_n),...  19.7 us
    pallas_call x1, Pallas kernels, body(): pl.pallas_call(functools.partial(scatter_kernel, plan), out_shape=jax.Sha...  18.7 us
    pallas_call x1, Pallas kernels, body(): pl.pallas_call(functools.partial(layers_kernel, depth_n, height_n), out_s...  12.2 us
    reshape x1, local copies, waits for them, and re-layouts, body(): volume.reshape(block)  1.22 us

profile of v1, /device:TPU:0, one launch (start us, length us, event | category | flops | bytes accessed | tf_op | source)
XLA Modules:
  0.0 58.0 jit_solution(2278732345856671816)
XLA Ops:
  0.6 0.8 %reshape.41 = f32[6912]{0:T(1024)S(1)} reshape(f32[2,3456]{1,0:T(2,128)} %param.7) | data formatting | bytes 55296 | tf_op jit(solution)/shard_map/reshape | solution.py:359
  1.4 0.0 copy-start
  1.4 1.2 %reshape.43.vol_ref = bf16[2,8,64,64]{3,2,1,0:T(8,128)(2,1)S(1)} reshape(bf16[1,2,8,4096]{3,2,1,0:T(8,128)(2,1)} %param.5) | data formatting | bytes 262144 | tf_op jit(solution)/shard_map/reshape | solution.py:382
  2.6 0.0 copy-done
  2.7 0.2 reshape.44.fg_ref
  2.9 19.7 %gather_kernels.1 = (bf16[32,64,128]{2,1,0:T(8,128)(2,1)S(1)}, bf16[4,8,64,192]{3,2,1,0:T(8,128)(2,1)S(1)}) custom-call(f32[64,128]{1,0:T(8,128)S(1)} %pad_bitcast_fusion.own_ref, bf16[2,8,64,64]{3,2,1,0:T(8,128)(2,1)S(1)} %reshape.43.vol_ref), custom_call_target="tpu_custom_call" | custom-call | tf_op jit(solution)/shard_map/gather_kernels/pallas_call | solution.py:363
  22.6 0.1 copy.11
  22.7 0.3 copy.12
  23.0 0.1 copy.13.kern_ref
  23.1 12.2 %two_layers.1 = (bf16[2,8,64,64]{3,2,1,0:T(8,128)(2,1)S(1)}, f32[2,864,128]{2,1,0:T(8,128)S(1)}) custom-call(bf16[4,8,64,192]{3,2,1,0:T(8,128)(2,1)S(1)} %get-tuple-element.8.wide_v, bf16[2,8,64,64]{3,2,1,0:T(8,128)(2,1)S(1)} %reshape.44.fg_ref, bf16[2,864,128]{2,1,0:T(8,128)(2,1)S(1)} %copy.13.kern_ref), custom_call_target="tpu_custom_call" | custom-call | tf_op jit(solution)/shard_map/two_layers/pallas_call | solution.py:396
  35.3 0.9 %reshape.47 = bf16[1,2,8,4096]{3,2,1,0:T(8,128)(2,1)} reshape(bf16[2,8,64,64]{3,2,1,0:T(8,128)(2,1)S(1)} %get-tuple-element.10) | data formatting | bytes 262144 | tf_op jit(solution)/shard_map/reshape | solution.py:420
  36.2 0.7 %copy.14 = f32[2,864,128]{2,0,1:T(2,128)S(1)} copy(f32[2,864,128]{2,1,0:T(8,128)S(1)} %get-tuple-element.11) | data formatting | bytes 1769472 | tf_op jit(solution)/shard_map/two_layers/pallas_call | solution.py:396
  36.9 0.2 copy.15
  37.1 0.5 copy.16
  37.7 0.1 pad.9.grads_ref
  37.8 0.0 copy-start.3
  37.8 18.7 %scatter_grads.1 = f32[64,128]{1,0:T(8,128)S(1)} custom-call(f32[32,64,128]{2,1,0:T(8,128)S(1)} %pad.9.grads_ref), custom_call_target="tpu_custom_call" | custom-call | tf_op jit(solution)/shard_map/scatter_grads/pallas_call | solution.py:430
  56.5 0.0 copy-start.1
  56.6 0.0 copy-start.2
  56.6 0.0 copy-done.3
  56.6 0.7 %copy-done.1 = f32[2,3456]{1,0:T(2,128)S(1)} copy-done((f32[2,3456]{1,0:T(2,128)S(1)}, f32[2,3456]{1,0:T(2,128)}, u32[]{:S(2)}) %copy-start.1) | copy-done | bytes 27672
  57.3 0.0 copy-done.2
  57.3 0.7 %divide_subtract_fusion = (f32[2,3456]{1,0:T(2,128)}, f32[2,3456]{1,0:T(2,128)}, f32[2,3456]{1,0:T(2,128)}) fusion(f32[2,3456]{1,0:T(2,128)S(1)} %copy-done.1, f32[2,3456]{1,0:T(2,128)S(1)} %reshape.50, f32[2,3456]{1,0:T(2,128)S(1)} %copy-done.2, f32[2,3456]{1,0:T(2,128)S(1)} %copy-done.3), kind=kLoop, calls=%fused_computation.3 | loop fusion | flops 82944 | bytes 193536 | tf_op jit(solution)/shard_map/sub | solution.py:453
  (4 shorter events, 0.1 us)
Async XLA Ops:
  1.4 1.2 %copy-start = (bf16[1,2,8,4096]{3,2,1,0:T(8,128)(2,1)S(1)}, bf16[1,2,8,4096]{3,2,1,0:T(8,128)(2,1)}, u32[]{:S(2)}) copy-start(bf16[1,2,8,4096]{3,2,1,0:T(8,128)(2,1)} %param.6) | copy-start | bytes 393220
  37.8 18.8 %copy-start.3 = (f32[2,3456]{1,0:T(2,128)S(1)}, f32[2,3456]{1,0:T(2,128)}, u32[]{:S(2)}) copy-start(f32[2,3456]{1,0:T(2,128)} %param.9) | copy-start | bytes 82948
  56.5 0.7 %copy-start.1 = (f32[2,3456]{1,0:T(2,128)S(1)}, f32[2,3456]{1,0:T(2,128)}, u32[]{:S(2)}) copy-start(f32[2,3456]{1,0:T(2,128)} %param.7) | copy-start | bytes 82948
  56.6 0.8 %copy-start.2 = (f32[2,3456]{1,0:T(2,128)S(1)}, f32[2,3456]{1,0:T(2,128)}, u32[]{:S(2)}) copy-start(f32[2,3456]{1,0:T(2,128)} %param.8) | copy-start | bytes 82948

commit v2 on v1

--- a/solution.py
+++ b/solution.py
@@ -23,99 +23,144 @@
 SIDES = [(a, b) for a in (-1, 0, 1) for b in (-1, 0, 1) if (a, b) != (0, 0)]
 
 
-def bit_plan(sizes):
-    dp, depth, height = sizes
-    plan = []
-    for k in range(height.bit_length() - 1):
-        plan.append((2, 1 << k))
-    for k in range(1, depth.bit_length() - 1):
-        plan.append((1, 1 << k))
-    for k in range(dp.bit_length() - 1):
-        plan.append((0, 1 << k))
-    plan.append((1, 1))
-    return plan
-
-
-def place_of(plan):
-    index = [lax.axis_index("dp"), lax.axis_index("depth"), lax.axis_index("height")]
-    bits, partners = [], []
-    for axis, unit in plan:
-        bit = lax.rem(index[axis] // unit, 2)
-        other = list(index)
-        other[axis] = index[axis] + (1 - 2 * bit) * unit
-        bits.append(bit)
-        partners.append(tuple(other))
-    return bits, partners
-
-
-def greet(partners):
-    barrier = pltpu.get_barrier_semaphore()
-    for partner in partners:
-        pl.semaphore_signal(barrier, inc=1, device_id=partner, device_id_type=MESH)
-    pl.semaphore_wait(barrier, len(partners))
+class Groups:
+    def __init__(self, sizes):
+        dp, depth, height = sizes
+        self.line, self.group = height, dp * (depth // 2)
+        self.half = self.line * self.group
+        p, d, h = lax.axis_index("dp"), lax.axis_index("depth"), lax.axis_index("height")
+        pairs = depth // 2
+        self.h, self.core = h, lax.rem(d, 2)
+        self.q = p * pairs + d // 2
+        self.start = self.core * self.half + self.q * self.line
+        self.in_line = [
+            (lax.rem(h + r, height), lax.rem(h + height - r, height)) for r in range(1, height)
+        ]
+        self.in_group = [
+            (lax.rem(self.q + r, self.group), lax.rem(self.q + self.group - r, self.group))
+            for r in range(1, self.group)
+        ]
+        self.line_ids = [(p, d, to) for to, _ in self.in_line]
+        self.group_ids = [
+            (to // pairs, 2 * lax.rem(to, pairs) + self.core, h) for to, _ in self.in_group
+        ]
+        self.core_id = (p, d + 1 - 2 * self.core, h)
+        self.ids = self.line_ids + self.group_ids + [self.core_id]
+
+    def greet(self):
+        barrier = pltpu.get_barrier_semaphore()
+        for other in self.ids:
+            pl.semaphore_signal(barrier, inc=1, device_id=other, device_id_type=MESH)
+        return barrier, len(self.ids)
 
 
 def gather_kernel(
-    plan, depth_n, height_n, own_ref, vol_ref, all_ref, wide_ref, vol, send_sem, recv_sem, side_send, side_recv
+    sizes,
+    own_ref,
+    vol_ref,
+    all_ref,
+    wide_ref,
+    vol,
+    send_sem,
+    recv_sem,
+    side_send,
+    side_recv,
 ):
-    bits, partners = place_of(plan)
-    place = sum(bit * (1 << k) for k, bit in enumerate(bits))
-    there, count, id_of = neighbours(depth_n, height_n)
+    at = Groups(sizes)
+    there, count, id_of = neighbours(sizes[1], sizes[2])
     clear_edges(vol)
     vol[pl.ds(1, vol_ref.shape[0]), pl.ds(1, vol_ref.shape[1])] = vol_ref[...]
-    all_ref[pl.ds(place, 1)] = own_ref[...].astype(BF)[None]
-    barrier = signal_neighbours(there, id_of)
-    for partner in partners:
-        pl.semaphore_signal(barrier, inc=1, device_id=partner, device_id_type=MESH)
-    pl.semaphore_wait(barrier, count + len(partners))
+    all_ref[pl.ds(at.start + at.h, 1)] = own_ref[...].astype(BF)[None]
+    barrier, partners = at.greet()
+    signal_neighbours(there, id_of)
+    pl.semaphore_wait(barrier, count + partners)
     halo = Halo(vol, there, id_of, side_send, side_recv)
-    for k, partner in enumerate(partners):
-        size = 1 << k
-        start = (place // size) * size
-        copy = pltpu.make_async_remote_copy(
-            src_ref=all_ref.at[pl.ds(start, size)],
-            dst_ref=all_ref.at[pl.ds(start, size)],
-            send_sem=send_sem.at[k],
-            recv_sem=recv_sem.at[k],
-            device_id=partner,
+
+    def copy_of(n, place, size):
+        part = all_ref.at[pl.ds(place, size)]
+        return pltpu.make_async_remote_copy(
+            src_ref=part,
+            dst_ref=part,
+            send_sem=send_sem.at[n],
+            recv_sem=recv_sem.at[n],
+            device_id=at.ids[n],
             device_id_type=MESH,
         )
-        copy.start()
-        if k == 0:
+
+    mine = at.core * at.half
+    others = (1 - at.core) * at.half
+    phases = [
+        [(at.start + at.h, at.start + source, 1) for _, source in at.in_line],
+        [(at.start, mine + source * at.line, at.line) for _, source in at.in_group],
+        [(mine, others, at.half)],
+    ]
+    first = 0
+    for number, phase in enumerate(phases):
+        for n, (out, _, size) in enumerate(phase):
+            copy_of(first + n, out, size).start()
+        if number == 0:
             halo.send()
-        if k == len(partners) - 1:
+        if number == 2:
             halo.arrive()
             widen(vol, wide_ref)
-        copy.wait()
+        for n, (_, source, size) in enumerate(phase):
+            copy_of(first + n, source, size).wait_recv()
+        first += len(phase)
+    first = 0
+    for phase in phases:
+        for n, (out, _, size) in enumerate(phase):
+            copy_of(first + n, out, size).wait_send()
+        first += len(phase)
     halo.sent()
 
 
-def scatter_kernel(plan, grads_ref, out_ref, acc, outgoing, incoming, send_sem, recv_sem):
-    bits, partners = place_of(plan)
-    greet(partners)
-    base = 0
-    for k in reversed(range(len(plan))):
-        size = 1 << k
-        source = grads_ref if k == len(plan) - 1 else acc
-        give = base + (1 - bits[k]) * size
-        keep = base + bits[k] * size
-        outgoing[pl.ds(size, size)] = source[pl.ds(give, size)].astype(BF)
-        copy = pltpu.make_async_remote_copy(
-            src_ref=outgoing.at[pl.ds(size, size)],
-            dst_ref=incoming.at[pl.ds(size, size)],
-            send_sem=send_sem.at[k],
-            recv_sem=recv_sem.at[k],
-            device_id=partners[k],
+def scatter_kernel(sizes, grads_ref, out_ref, acc, outgoing, incoming, send_sem, recv_sem):
+    at = Groups(sizes)
+    barrier, partners = at.greet()
+    line, half = at.line, at.half
+
+    def copy_of(n, source, place, size):
+        return pltpu.make_async_remote_copy(
+            src_ref=outgoing.at[pl.ds(source, size)],
+            dst_ref=incoming.at[pl.ds(place, size)],
+            send_sem=send_sem.at[n],
+            recv_sem=recv_sem.at[n],
+            device_id=at.ids[n],
             device_id_type=MESH,
         )
-        copy.start()
-        copy.wait()
-        total = source[pl.ds(keep, size)] + incoming[pl.ds(size, size)].astype(F32)
-        if k:
-            acc[pl.ds(keep, size)] = total
-        else:
-            out_ref[...] = total[0]
-        base = keep
+
+    last = len(at.ids) - 1
+    outgoing[pl.ds(half, half)] = grads_ref[pl.ds((1 - at.core) * half, half)].astype(BF)
+    pl.semaphore_wait(barrier, partners)
+    across = copy_of(last, half, half, half)
+    across.start()
+    across.wait_recv()
+    total = grads_ref[pl.ds(at.core * half, half)] + incoming[pl.ds(half, half)].astype(F32)
+    acc[...] = total
+    outgoing[pl.ds(0, half)] = total.astype(BF)
+    first = len(at.in_line)
+    copies = [across]
+    group = []
+    for n, (to, _) in enumerate(at.in_group):
+        group.append(copy_of(first + n, to * line, (n + 1) * line, line))
+        group[-1].start()
+    total = acc[pl.ds(at.q * line, line)]
+    for n, copy in enumerate(group):
+        copy.wait_recv()
+        total = total + incoming[pl.ds((n + 1) * line, line)].astype(F32)
+    acc[pl.ds(at.q * line, line)] = total
+    outgoing[pl.ds(at.q * line, line)] = total.astype(BF)
+    final = []
+    for n, (to, _) in enumerate(at.in_line):
+        final.append(copy_of(n, at.q * line + to, n + 1, 1))
+        final[-1].start()
+    total = acc[pl.ds(at.q * line + at.h, 1)]
+    for n, copy in enumerate(final):
+        copy.wait_recv()
+        total = total + incoming[pl.ds(n + 1, 1)].astype(F32)
+    out_ref[...] = total[0]
+    for copy in copies + group + final:
+        copy.wait_send()
 
 
 def span(side, cells, arriving):
@@ -349,8 +394,7 @@
 def body(sizes, volume, feature_grad, master_weights, first_moment, second_moment):
     dp_n, depth_n, height_n = sizes
     devices = dp_n * depth_n * height_n
-    plan = bit_plan(sizes)
-    steps = len(plan)
+    steps = (height_n - 1) + (dp_n * (depth_n // 2) - 1) + 1
     cells_d, cells_h = volume.shape[1], volume.shape[2]
     shard = master_weights.shape[1]
     slot_rows = -(-2 * shard // (16 * 128)) * 16
@@ -361,7 +405,7 @@
     padded = (cells_d + 2, cells_h + 2, WIDTH, C)
     wide = (cells_d + 2, cells_h, WIDTH, 3 * C)
     gathered, wide_volume = pl.pallas_call(
-        functools.partial(gather_kernel, plan, depth_n, height_n),
+        functools.partial(gather_kernel, sizes),
         out_shape=(
             jax.ShapeDtypeStruct((devices, slot_rows, 128), BF),
             jax.ShapeDtypeStruct(wide, BF),
@@ -428,12 +472,12 @@
         parts = jnp.pad(parts.reshape(devices, 2 * shard), ((0, 0), (0, pad)))
         parts = parts.reshape(devices, slot_rows, 128)
     summed = pl.pallas_call(
-        functools.partial(scatter_kernel, plan),
+        functools.partial(scatter_kernel, sizes),
         out_shape=jax.ShapeDtypeStruct((slot_rows, 128), F32),
         in_specs=vmem(1),
         out_specs=vmem(1)[0],
         scratch_shapes=[
-            pltpu.VMEM((devices, slot_rows, 128), F32),
+            pltpu.VMEM((devices // 2, slot_rows, 128), F32),
             pltpu.VMEM((devices, slot_rows, 128), BF),
             pltpu.VMEM((devices, slot_rows, 128), BF),
             pltpu.SemaphoreType.DMA((steps,)),

time: 58.3 us -> 47.6 us (0.82)
  Pallas kernels: 50.6 us -> 39.9 us
    pallas_call x2, Pallas kernels: 38.4 us -> 27.7 us  [the longest x1 14.4 us: body(): pl.pallas_call(functools.partial(gather_kernel, sizes), out_shape=(jax.Sh...]
where the time goes in v2:
time: 47.6 us; the launch traced here: 47.3 us
  Pallas kernels  39.9 us (84%)
  local copies, waits for them, and re-layouts  5.97 us (13%)
  between operations  0.79 us (2%)
  other arithmetic  0.71 us (1%)
    pallas_call x1, Pallas kernels, body(): pl.pallas_call(functools.partial(gather_kernel, sizes), out_shape=(jax.Sh...  14.4 us
    pallas_call x1, Pallas kernels, body(): pl.pallas_call(functools.partial(scatter_kernel, sizes), out_shape=jax.Sh...  13.3 us
    pallas_call x1, Pallas kernels, body(): pl.pallas_call(functools.partial(layers_kernel, depth_n, height_n), out_s...  12.1 us
    reshape x1, local copies, waits for them, and re-layouts, body(): volume.reshape(block)  1.22 us

profile of v2, /device:TPU:0, one launch (start us, length us, event | category | flops | bytes accessed | tf_op | source)
XLA Modules:
  0.0 47.3 jit_solution(1963033892754562545)
XLA Ops:
  0.6 0.8 %reshape.41 = f32[6912]{0:T(1024)S(1)} reshape(f32[2,3456]{1,0:T(2,128)} %param.7) | data formatting | bytes 55296 | tf_op jit(solution)/shard_map/reshape | solution.py:403
  1.4 0.0 copy-start
  1.4 1.2 %reshape.43.vol_ref = bf16[2,8,64,64]{3,2,1,0:T(8,128)(2,1)S(1)} reshape(bf16[1,2,8,4096]{3,2,1,0:T(8,128)(2,1)} %param.5) | data formatting | bytes 262144 | tf_op jit(solution)/shard_map/reshape | solution.py:426
  2.6 0.0 copy-done
  2.7 0.2 reshape.44.fg_ref
  2.9 14.4 %gather_kernels.1 = (bf16[32,64,128]{2,1,0:T(8,128)(2,1)S(1)}, bf16[4,8,64,192]{3,2,1,0:T(8,128)(2,1)S(1)}) custom-call(f32[64,128]{1,0:T(8,128)S(1)} %pad_bitcast_fusion.own_ref, bf16[2,8,64,64]{3,2,1,0:T(8,128)(2,1)S(1)} %reshape.43.vol_ref), custom_call_target="tpu_custom_call" | custom-call | tf_op jit(solution)/shard_map/gather_kernels/pallas_call | solution.py:407
  17.4 0.1 copy.11
  17.5 0.3 copy.12
  17.8 0.1 copy.13.kern_ref
  17.9 12.1 %two_layers.1 = (bf16[2,8,64,64]{3,2,1,0:T(8,128)(2,1)S(1)}, f32[2,864,128]{2,1,0:T(8,128)S(1)}) custom-call(bf16[4,8,64,192]{3,2,1,0:T(8,128)(2,1)S(1)} %get-tuple-element.8.wide_v, bf16[2,8,64,64]{3,2,1,0:T(8,128)(2,1)S(1)} %reshape.44.fg_ref, bf16[2,864,128]{2,1,0:T(8,128)(2,1)S(1)} %copy.13.kern_ref), custom_call_target="tpu_custom_call" | custom-call | tf_op jit(solution)/shard_map/two_layers/pallas_call | solution.py:440
  30.0 0.9 %reshape.47 = bf16[1,2,8,4096]{3,2,1,0:T(8,128)(2,1)} reshape(bf16[2,8,64,64]{3,2,1,0:T(8,128)(2,1)S(1)} %get-tuple-element.10) | data formatting | bytes 262144 | tf_op jit(solution)/shard_map/reshape | solution.py:464
  31.0 0.7 %copy.14 = f32[2,864,128]{2,0,1:T(2,128)S(1)} copy(f32[2,864,128]{2,1,0:T(8,128)S(1)} %get-tuple-element.11) | data formatting | bytes 1769472 | tf_op jit(solution)/shard_map/two_layers/pallas_call | solution.py:440
  31.7 0.2 copy.15
  31.9 0.5 %copy.16 = f32[32,54,128]{2,1,0:T(8,128)S(1)} copy(f32[32,54,128]{2,0,1:T(8,128)S(1)} %bitcast.17) | data formatting | bytes 1769472 | tf_op jit(solution)/shard_map/reshape | solution.py:469
  32.4 0.1 pad.9.grads_ref
  32.5 0.0 copy-start.3
  32.6 13.3 %scatter_grads.1 = f32[64,128]{1,0:T(8,128)S(1)} custom-call(f32[32,64,128]{2,1,0:T(8,128)S(1)} %pad.9.grads_ref), custom_call_target="tpu_custom_call" | custom-call | tf_op jit(solution)/shard_map/scatter_grads/pallas_call | solution.py:474
  45.9 0.0 copy-start.1
  45.9 0.0 copy-start.2
  45.9 0.0 copy-done.3
  45.9 0.7 %copy-done.1 = f32[2,3456]{1,0:T(2,128)S(1)} copy-done((f32[2,3456]{1,0:T(2,128)S(1)}, f32[2,3456]{1,0:T(2,128)}, u32[]{:S(2)}) %copy-start.1) | copy-done | bytes 27672
  46.6 0.0 copy-done.2
  46.6 0.7 %divide_subtract_fusion = (f32[2,3456]{1,0:T(2,128)}, f32[2,3456]{1,0:T(2,128)}, f32[2,3456]{1,0:T(2,128)}) fusion(f32[2,3456]{1,0:T(2,128)S(1)} %copy-done.1, f32[2,3456]{1,0:T(2,128)S(1)} %reshape.50, f32[2,3456]{1,0:T(2,128)S(1)} %copy-done.2, f32[2,3456]{1,0:T(2,128)S(1)} %copy-done.3), kind=kLoop, calls=%fused_computation.3 | loop fusion | flops 82944 | bytes 193536 | tf_op jit(solution)/shard_map/sub | solution.py:497
  (4 shorter events, 0.1 us)
Async XLA Ops:
  1.4 1.2 %copy-start = (bf16[1,2,8,4096]{3,2,1,0:T(8,128)(2,1)S(1)}, bf16[1,2,8,4096]{3,2,1,0:T(8,128)(2,1)}, u32[]{:S(2)}) copy-start(bf16[1,2,8,4096]{3,2,1,0:T(8,128)(2,1)} %param.6) | copy-start | bytes 393220
  32.5 13.4 %copy-start.3 = (f32[2,3456]{1,0:T(2,128)S(1)}, f32[2,3456]{1,0:T(2,128)}, u32[]{:S(2)}) copy-start(f32[2,3456]{1,0:T(2,128)} %param.9) | copy-start | bytes 82948
  45.9 0.7 %copy-start.1 = (f32[2,3456]{1,0:T(2,128)S(1)}, f32[2,3456]{1,0:T(2,128)}, u32[]{:S(2)}) copy-start(f32[2,3456]{1,0:T(2,128)} %param.7) | copy-start | bytes 82948
  45.9 0.8 %copy-start.2 = (f32[2,3456]{1,0:T(2,128)S(1)}, f32[2,3456]{1,0:T(2,128)}, u32[]{:S(2)}) copy-start(f32[2,3456]{1,0:T(2,128)} %param.8) | copy-start | bytes 82948

commit v3 on v2

--- a/solution.py
+++ b/solution.py
@@ -46,6 +46,7 @@
         ]
         self.core_id = (p, d + 1 - 2 * self.core, h)
         self.ids = self.line_ids + self.group_ids + [self.core_id]
+        self.peers = self.line_ids + self.group_ids + [self.core_id] * self.group
 
     def greet(self):
         barrier = pltpu.get_barrier_semaphore()
@@ -83,34 +84,38 @@
             dst_ref=part,
             send_sem=send_sem.at[n],
             recv_sem=recv_sem.at[n],
-            device_id=at.ids[n],
+            device_id=at.peers[n],
             device_id_type=MESH,
         )
 
     mine = at.core * at.half
     others = (1 - at.core) * at.half
-    phases = [
-        [(at.start + at.h, at.start + source, 1) for _, source in at.in_line],
-        [(at.start, mine + source * at.line, at.line) for _, source in at.in_group],
-        [(mine, others, at.half)],
-    ]
-    first = 0
-    for number, phase in enumerate(phases):
-        for n, (out, _, size) in enumerate(phase):
-            copy_of(first + n, out, size).start()
-        if number == 0:
-            halo.send()
-        if number == 2:
-            halo.arrive()
-            widen(vol, wide_ref)
-        for n, (_, source, size) in enumerate(phase):
-            copy_of(first + n, source, size).wait_recv()
-        first += len(phase)
-    first = 0
-    for phase in phases:
-        for n, (out, _, size) in enumerate(phase):
-            copy_of(first + n, out, size).wait_send()
-        first += len(phase)
+    line = at.line
+    sent = []
+
+    def start(n, place, size):
+        sent.append(copy_of(n, place, size))
+        sent[-1].start()
+
+    for n in range(len(at.in_line)):
+        start(n, at.start + at.h, 1)
+    halo.send()
+    for n, (_, source) in enumerate(at.in_line):
+        copy_of(n, at.start + source, 1).wait_recv()
+    first = len(at.in_line)
+    core = first + len(at.in_group)
+    for n in range(len(at.in_group)):
+        start(first + n, at.start, line)
+    start(core, at.start, line)
+    for n, (_, source) in enumerate(at.in_group):
+        copy_of(first + n, mine + source * line, line).wait_recv()
+        start(core + 1 + n, mine + source * line, line)
+    halo.arrive()
+    widen(vol, wide_ref)
+    for n, source in enumerate([at.q] + [source for _, source in at.in_group]):
+        copy_of(core + n, others + source * line, line).wait_recv()
+    for copy in sent:
+        copy.wait_send()
     halo.sent()
 
 
@@ -125,41 +130,45 @@
             dst_ref=incoming.at[pl.ds(place, size)],
             send_sem=send_sem.at[n],
             recv_sem=recv_sem.at[n],
-            device_id=at.ids[n],
+            device_id=at.peers[n],
             device_id_type=MESH,
         )
 
-    last = len(at.ids) - 1
-    outgoing[pl.ds(half, half)] = grads_ref[pl.ds((1 - at.core) * half, half)].astype(BF)
+    first = len(at.in_line)
+    core = first + len(at.in_group)
+    order = [to for to, _ in at.in_group] + [at.q]
+    keep, give = at.core * half, (1 - at.core) * half
     pl.semaphore_wait(barrier, partners)
-    across = copy_of(last, half, half, half)
-    across.start()
-    across.wait_recv()
-    total = grads_ref[pl.ds(at.core * half, half)] + incoming[pl.ds(half, half)].astype(F32)
-    acc[...] = total
-    outgoing[pl.ds(0, half)] = total.astype(BF)
-    first = len(at.in_line)
-    copies = [across]
+    across = []
+    for n, to in enumerate(order):
+        there = half + to * line
+        outgoing[pl.ds(there, line)] = grads_ref[pl.ds(give + to * line, line)].astype(BF)
+        across.append(copy_of(core + n, there, there, line))
+        across[-1].start()
     group = []
-    for n, (to, _) in enumerate(at.in_group):
-        group.append(copy_of(first + n, to * line, (n + 1) * line, line))
-        group[-1].start()
-    total = acc[pl.ds(at.q * line, line)]
+    for n, to in enumerate(order):
+        across[n].wait_recv()
+        total = grads_ref[pl.ds(keep + to * line, line)]
+        total = total + incoming[pl.ds(half + to * line, line)].astype(F32)
+        if n < len(at.in_group):
+            outgoing[pl.ds(to * line, line)] = total.astype(BF)
+            group.append(copy_of(first + n, to * line, (n + 1) * line, line))
+            group[-1].start()
     for n, copy in enumerate(group):
         copy.wait_recv()
         total = total + incoming[pl.ds((n + 1) * line, line)].astype(F32)
-    acc[pl.ds(at.q * line, line)] = total
+    acc[...] = total
     outgoing[pl.ds(at.q * line, line)] = total.astype(BF)
     final = []
     for n, (to, _) in enumerate(at.in_line):
         final.append(copy_of(n, at.q * line + to, n + 1, 1))
         final[-1].start()
-    total = acc[pl.ds(at.q * line + at.h, 1)]
+    total = acc[pl.ds(at.h, 1)]
     for n, copy in enumerate(final):
         copy.wait_recv()
         total = total + incoming[pl.ds(n + 1, 1)].astype(F32)
     out_ref[...] = total[0]
-    for copy in copies + group + final:
+    for copy in across + group + final:
         copy.wait_send()
 
 
@@ -251,6 +260,7 @@
 def layers_kernel(
     depth_n,
     height_n,
+    slot_of,
     wide_v,
     fg_ref,
     kern_ref,
@@ -269,6 +279,10 @@
     cells_d, cells_h = fg_ref.shape[0], fg_ref.shape[1]
     line = cells_h * WIDTH
     there, count, id_of = neighbours(depth_n, height_n)
+    if slot_of is not None:
+        used = 2 * slot_of[1]
+        spare = (grad_ref.shape[0], grad_ref.shape[1] - used, 128)
+        grad_ref[:, pl.ds(used, spare[1])] = jnp.zeros(spare, F32)
     clear_edges(hid)
     clear_edges(del2)
     barrier = signal_neighbours(there, id_of)
@@ -337,9 +351,19 @@
             for b in range(3):
                 for c in range(3):
                     part = (slice(b * half, (b + 1) * half), slice(c % 2 * C, (c % 2 + 1) * C))
-                    grad_ref[layer, pl.ds((9 * a + 3 * b + c) * half, half)] = jnp.concatenate(
-                        [even[c // 2][part], odd[c // 2][part]], 1
-                    )
+                    tap = jnp.concatenate([even[c // 2][part], odd[c // 2][part]], 1)
+                    row = (9 * a + 3 * b + c) * half
+                    if slot_of is None:
+                        grad_ref[layer, pl.ds(row, half)] = tap
+                        continue
+                    at, share = 0, slot_of[1]
+                    while at < half:
+                        owner, skip = divmod(row + at, share)
+                        size = min(half - at, share - skip)
+                        grad_ref[slot_of[0][owner], pl.ds(layer * share + skip, size)] = tap[
+                            at : at + size
+                        ]
+                        at += size
 
     for d in range(cells_d):
         linear = conv(wide_v, 0, d)
@@ -394,7 +418,7 @@
 def body(sizes, volume, feature_grad, master_weights, first_moment, second_moment):
     dp_n, depth_n, height_n = sizes
     devices = dp_n * depth_n * height_n
-    steps = (height_n - 1) + (dp_n * (depth_n // 2) - 1) + 1
+    steps = (height_n - 1) + 2 * dp_n * (depth_n // 2) - 1
     cells_d, cells_h = volume.shape[1], volume.shape[2]
     shard = master_weights.shape[1]
     slot_rows = -(-2 * shard // (16 * 128)) * 16
@@ -437,11 +461,19 @@
         .reshape(2, devices * shard // 128, 128)
     )
 
+    slot_of, grads_shape = None, kernels.shape
+    if len(unit) == 2 and slot_rows > 2 * unit[0]:
+        places = []
+        for device in range(devices):
+            p, d, h = device // (depth_n * height_n), device // height_n % depth_n, device % height_n
+            places.append(((d % 2 * dp_n + p) * (depth_n // 2) + d // 2) * height_n + h)
+        slot_of, grads_shape = (places, unit[0]), (devices, slot_rows, 128)
+
     features, grads = pl.pallas_call(
-        functools.partial(layers_kernel, depth_n, height_n),
+        functools.partial(layers_kernel, depth_n, height_n, slot_of),
         out_shape=(
             jax.ShapeDtypeStruct(block, BF),
-            jax.ShapeDtypeStruct(kernels.shape, F32),
+            jax.ShapeDtypeStruct(grads_shape, F32),
         ),
         in_specs=vmem(3),
         out_specs=tuple(vmem(2)),
@@ -464,8 +496,11 @@
     features = features.reshape(1, cells_d, cells_h, WIDTH * C)
 
     order = (3, 1, 2, 4, 0) + tuple(range(5, 5 + len(unit)))
-    parts = grads.reshape((2, dp_n, depth_n // 2, 2, height_n) + unit).transpose(order)
-    if len(unit) == 2:
+    if slot_of is None:
+        parts = grads.reshape((2, dp_n, depth_n // 2, 2, height_n) + unit).transpose(order)
+    if slot_of is not None:
+        parts = grads
+    elif len(unit) == 2:
         parts = parts.reshape(devices, 2 * unit[0], 128)
         parts = jnp.pad(parts, ((0, 0), (0, slot_rows - 2 * unit[0]), (0, 0)))
     else:
@@ -477,7 +512,7 @@
         in_specs=vmem(1),
         out_specs=vmem(1)[0],
         scratch_shapes=[
-            pltpu.VMEM((devices // 2, slot_rows, 128), F32),
+            pltpu.VMEM((height_n, slot_rows, 128), F32),
             pltpu.VMEM((devices, slot_rows, 128), BF),
             pltpu.VMEM((devices, slot_rows, 128), BF),
             pltpu.SemaphoreType.DMA((steps,)),

time: 47.6 us -> 45.6 us (0.958)
  local copies, waits for them, and re-layouts: 5.97 us -> 4.42 us
    pallas_call x1 -> x0, local copies, waits for them, and re-layouts: 0.68 us -> none  [body(): pl.pallas_call(functools.partial(layers_kernel, depth_n, height_n), out_s...]
    reshape x1 -> x0, local copies, waits for them, and re-layouts: 0.52 us -> none  [body(): parts = parts.reshape(devices, 2 * unit[0], 128)]
where the time goes in v3:
time: 45.6 us; the launch traced here: 45.4 us
  Pallas kernels  39.5 us (87%)
  local copies, waits for them, and re-layouts  4.42 us (10%)
  between operations  0.76 us (2%)
  other arithmetic  0.71 us (2%)
    pallas_call x1, Pallas kernels, body(): pl.pallas_call(functools.partial(gather_kernel, sizes), out_shape=(jax.Sh...  14.3 us
    pallas_call x1, Pallas kernels, body(): pl.pallas_call(functools.partial(scatter_kernel, sizes), out_shape=jax.Sh...  12.9 us
    pallas_call x1, Pallas kernels, body(): pl.pallas_call(functools.partial(layers_kernel, depth_n, height_n, slot_o...  12.3 us
    reshape x1, local copies, waits for them, and re-layouts, body(): volume.reshape(block)  1.22 us
    reshape x1, local copies, waits for them, and re-layouts, body(): features = features.reshape(1, cells_d, cells_h, WIDTH * C)  0.93 us

profile of v3, /device:TPU:0, one launch (start us, length us, event | category | flops | bytes accessed | tf_op | source)
XLA Modules:
  0.0 45.4 jit_solution(1154836449516866305)
XLA Ops:
  0.6 0.8 %reshape.35 = f32[6912]{0:T(1024)S(1)} reshape(f32[2,3456]{1,0:T(2,128)} %param.7) | data formatting | bytes 55296 | tf_op jit(solution)/shard_map/reshape | solution.py:427
  1.4 0.0 copy-start
  1.4 1.2 %reshape.37.vol_ref = bf16[2,8,64,64]{3,2,1,0:T(8,128)(2,1)S(1)} reshape(bf16[1,2,8,4096]{3,2,1,0:T(8,128)(2,1)} %param.5) | data formatting | bytes 262144 | tf_op jit(solution)/shard_map/reshape | solution.py:450
  2.6 0.0 copy-done
  2.7 0.2 reshape.38.fg_ref
  2.9 14.3 %gather_kernels.1 = (bf16[32,64,128]{2,1,0:T(8,128)(2,1)S(1)}, bf16[4,8,64,192]{3,2,1,0:T(8,128)(2,1)S(1)}) custom-call(f32[64,128]{1,0:T(8,128)S(1)} %pad_bitcast_fusion.own_ref, bf16[2,8,64,64]{3,2,1,0:T(8,128)(2,1)S(1)} %reshape.37.vol_ref), custom_call_target="tpu_custom_call" | custom-call | tf_op jit(solution)/shard_map/gather_kernels/pallas_call | solution.py:431
  17.2 0.1 copy.10
  17.3 0.3 copy.11
  17.7 0.1 copy.12.kern_ref
  17.7 12.3 %two_layers.1 = (bf16[2,8,64,64]{3,2,1,0:T(8,128)(2,1)S(1)}, f32[32,64,128]{2,1,0:T(8,128)S(1)}) custom-call(bf16[4,8,64,192]{3,2,1,0:T(8,128)(2,1)S(1)} %get-tuple-element.8.wide_v, bf16[2,8,64,64]{3,2,1,0:T(8,128)(2,1)S(1)} %reshape.38.fg_ref, bf16[2,864,128]{2,1,0:T(8,128)(2,1)S(1)} %copy.12.kern_ref), custom_call_target="tpu_custom_call" | custom-call | tf_op jit(solution)/shard_map/two_layers/pallas_call | solution.py:472
  30.0 0.9 %reshape.41 = bf16[1,2,8,4096]{3,2,1,0:T(8,128)(2,1)} reshape(bf16[2,8,64,64]{3,2,1,0:T(8,128)(2,1)S(1)} %get-tuple-element.10) | data formatting | bytes 262144 | tf_op jit(solution)/shard_map/reshape | solution.py:496
  30.9 0.0 copy-start.3
  30.9 12.9 %scatter_grads.1 = f32[64,128]{1,0:T(8,128)S(1)} custom-call(f32[32,64,128]{2,1,0:T(8,128)S(1)} %get-tuple-element.11.grads_ref), custom_call_target="tpu_custom_call" | custom-call | tf_op jit(solution)/shard_map/scatter_grads/pallas_call | solution.py:509
  43.9 0.0 copy-start.1
  43.9 0.0 copy-start.2
  44.0 0.0 copy-done.3
  44.0 0.7 %copy-done.1 = f32[2,3456]{1,0:T(2,128)S(1)} copy-done((f32[2,3456]{1,0:T(2,128)S(1)}, f32[2,3456]{1,0:T(2,128)}, u32[]{:S(2)}) %copy-start.1) | copy-done | bytes 27672
  44.7 0.0 copy-done.2
  44.7 0.7 %divide_subtract_fusion = (f32[2,3456]{1,0:T(2,128)}, f32[2,3456]{1,0:T(2,128)}, f32[2,3456]{1,0:T(2,128)}) fusion(f32[2,3456]{1,0:T(2,128)S(1)} %copy-done.1, f32[2,3456]{1,0:T(2,128)S(1)} %reshape.42, f32[2,3456]{1,0:T(2,128)S(1)} %copy-done.2, f32[2,3456]{1,0:T(2,128)S(1)} %copy-done.3), kind=kLoop, calls=%fused_computation.3 | loop fusion | flops 82944 | bytes 193536 | tf_op jit(solution)/shard_map/sub | solution.py:532
  (4 shorter events, 0.1 us)
Async XLA Ops:
  1.4 1.2 %copy-start = (bf16[1,2,8,4096]{3,2,1,0:T(8,128)(2,1)S(1)}, bf16[1,2,8,4096]{3,2,1,0:T(8,128)(2,1)}, u32[]{:S(2)}) copy-start(bf16[1,2,8,4096]{3,2,1,0:T(8,128)(2,1)} %param.6) | copy-start | bytes 393220
  30.9 13.0 %copy-start.3 = (f32[2,3456]{1,0:T(2,128)S(1)}, f32[2,3456]{1,0:T(2,128)}, u32[]{:S(2)}) copy-start(f32[2,3456]{1,0:T(2,128)} %param.9) | copy-start | bytes 82948
  43.9 0.7 %copy-start.1 = (f32[2,3456]{1,0:T(2,128)S(1)}, f32[2,3456]{1,0:T(2,128)}, u32[]{:S(2)}) copy-start(f32[2,3456]{1,0:T(2,128)} %param.7) | copy-start | bytes 82948
  43.9 0.8 %copy-start.2 = (f32[2,3456]{1,0:T(2,128)S(1)}, f32[2,3456]{1,0:T(2,128)}, u32[]{:S(2)}) copy-start(f32[2,3456]{1,0:T(2,128)} %param.8) | copy-start | bytes 82948

commit v4 on v3

--- a/solution.py
+++ b/solution.py
@@ -288,7 +288,7 @@
     barrier = signal_neighbours(there, id_of)
 
     half = C // 2
-    for layer in range(2):
+    def assemble(layer):
         for a in range(3):
             for b in range(3):
                 taps = [
@@ -303,6 +303,7 @@
             weights[layer, a, :, 0 : 2 * C] = mixed[a, 0].astype(BF)
             weights[layer, a, :, 2 * C : 3 * C] = mixed[a, 1, :, 0:C].astype(BF)
 
+    assemble(0)
     pl.semaphore_wait(barrier, count)
     hid_halo = Halo(hid, there, id_of, send_sem.at[0], recv_sem.at[0])
     del_halo = Halo(del2, there, id_of, send_sem.at[1], recv_sem.at[1])
@@ -371,6 +372,7 @@
         slope1[d] = slope
         hid[d + 1, pl.ds(1, cells_h)] = (linear * slope).astype(BF).reshape(cells_h, WIDTH, C)
     hid_halo.send()
+    assemble(1)
     hid_halo.arrive()
     widen(hid, wide_h)
     for d in range(cells_d):

time: 45.6 us -> 45.6 us (level)
  no operation moved by 1% of the time
where the time goes in v4:
time: 45.6 us; the launch traced here: 45.4 us
  Pallas kernels  39.5 us (87%)
  local copies, waits for them, and re-layouts  4.42 us (10%)
  between operations  0.76 us (2%)
  other arithmetic  0.71 us (2%)
    pallas_call x1, Pallas kernels, body(): pl.pallas_call(functools.partial(gather_kernel, sizes), out_shape=(jax.Sh...  14.3 us
    pallas_call x1, Pallas kernels, body(): pl.pallas_call(functools.partial(scatter_kernel, sizes), out_shape=jax.Sh...  12.9 us
    pallas_call x1, Pallas kernels, body(): pl.pallas_call(functools.partial(layers_kernel, depth_n, height_n, slot_o...  12.3 us
    reshape x1, local copies, waits for them, and re-layouts, body(): volume.reshape(block)  1.22 us
    reshape x1, local copies, waits for them, and re-layouts, body(): features = features.reshape(1, cells_d, cells_h, WIDTH * C)  0.93 us

profile of v4, /device:TPU:0, one launch (start us, length us, event | category | flops | bytes accessed | tf_op | source)
XLA Modules:
  0.0 45.4 jit_solution(6878260780892117671)
XLA Ops:
  0.6 0.8 %reshape.35 = f32[6912]{0:T(1024)S(1)} reshape(f32[2,3456]{1,0:T(2,128)} %param.7) | data formatting | bytes 55296 | tf_op jit(solution)/shard_map/reshape | solution.py:429
  1.4 0.0 copy-start
  1.4 1.2 %reshape.37.vol_ref = bf16[2,8,64,64]{3,2,1,0:T(8,128)(2,1)S(1)} reshape(bf16[1,2,8,4096]{3,2,1,0:T(8,128)(2,1)} %param.5) | data formatting | bytes 262144 | tf_op jit(solution)/shard_map/reshape | solution.py:452
  2.6 0.0 copy-done
  2.7 0.2 reshape.38.fg_ref
  2.9 14.3 %gather_kernels.1 = (bf16[32,64,128]{2,1,0:T(8,128)(2,1)S(1)}, bf16[4,8,64,192]{3,2,1,0:T(8,128)(2,1)S(1)}) custom-call(f32[64,128]{1,0:T(8,128)S(1)} %pad_bitcast_fusion.own_ref, bf16[2,8,64,64]{3,2,1,0:T(8,128)(2,1)S(1)} %reshape.37.vol_ref), custom_call_target="tpu_custom_call" | custom-call | tf_op jit(solution)/shard_map/gather_kernels/pallas_call | solution.py:433
  17.2 0.1 copy.10
  17.3 0.3 copy.11
  17.7 0.1 copy.12.kern_ref
  17.7 12.3 %two_layers.1 = (bf16[2,8,64,64]{3,2,1,0:T(8,128)(2,1)S(1)}, f32[32,64,128]{2,1,0:T(8,128)S(1)}) custom-call(bf16[4,8,64,192]{3,2,1,0:T(8,128)(2,1)S(1)} %get-tuple-element.8.wide_v, bf16[2,8,64,64]{3,2,1,0:T(8,128)(2,1)S(1)} %reshape.38.fg_ref, bf16[2,864,128]{2,1,0:T(8,128)(2,1)S(1)} %copy.12.kern_ref), custom_call_target="tpu_custom_call" | custom-call | tf_op jit(solution)/shard_map/two_layers/pallas_call | solution.py:474
  30.0 0.9 %reshape.41 = bf16[1,2,8,4096]{3,2,1,0:T(8,128)(2,1)} reshape(bf16[2,8,64,64]{3,2,1,0:T(8,128)(2,1)S(1)} %get-tuple-element.10) | data formatting | bytes 262144 | tf_op jit(solution)/shard_map/reshape | solution.py:498
  30.9 0.0 copy-start.3
  30.9 12.9 %scatter_grads.1 = f32[64,128]{1,0:T(8,128)S(1)} custom-call(f32[32,64,128]{2,1,0:T(8,128)S(1)} %get-tuple-element.11.grads_ref), custom_call_target="tpu_custom_call" | custom-call | tf_op jit(solution)/shard_map/scatter_grads/pallas_call | solution.py:511
  43.9 0.0 copy-start.1
  43.9 0.0 copy-start.2
  44.0 0.0 copy-done.3
  44.0 0.7 %copy-done.1 = f32[2,3456]{1,0:T(2,128)S(1)} copy-done((f32[2,3456]{1,0:T(2,128)S(1)}, f32[2,3456]{1,0:T(2,128)}, u32[]{:S(2)}) %copy-start.1) | copy-done | bytes 27672
  44.7 0.0 copy-done.2
  44.7 0.7 %divide_subtract_fusion = (f32[2,3456]{1,0:T(2,128)}, f32[2,3456]{1,0:T(2,128)}, f32[2,3456]{1,0:T(2,128)}) fusion(f32[2,3456]{1,0:T(2,128)S(1)} %copy-done.1, f32[2,3456]{1,0:T(2,128)S(1)} %reshape.42, f32[2,3456]{1,0:T(2,128)S(1)} %copy-done.2, f32[2,3456]{1,0:T(2,128)S(1)} %copy-done.3), kind=kLoop, calls=%fused_computation.3 | loop fusion | flops 82944 | bytes 193536 | tf_op jit(solution)/shard_map/sub | solution.py:534
  (4 shorter events, 0.1 us)
Async XLA Ops:
  1.4 1.2 %copy-start = (bf16[1,2,8,4096]{3,2,1,0:T(8,128)(2,1)S(1)}, bf16[1,2,8,4096]{3,2,1,0:T(8,128)(2,1)}, u32[]{:S(2)}) copy-start(bf16[1,2,8,4096]{3,2,1,0:T(8,128)(2,1)} %param.6) | copy-start | bytes 393220
  30.9 13.0 %copy-start.3 = (f32[2,3456]{1,0:T(2,128)S(1)}, f32[2,3456]{1,0:T(2,128)}, u32[]{:S(2)}) copy-start(f32[2,3456]{1,0:T(2,128)} %param.9) | copy-start | bytes 82948
  43.9 0.7 %copy-start.1 = (f32[2,3456]{1,0:T(2,128)S(1)}, f32[2,3456]{1,0:T(2,128)}, u32[]{:S(2)}) copy-start(f32[2,3456]{1,0:T(2,128)} %param.7) | copy-start | bytes 82948
  43.9 0.8 %copy-start.2 = (f32[2,3456]{1,0:T(2,128)S(1)}, f32[2,3456]{1,0:T(2,128)}, u32[]{:S(2)}) copy-start(f32[2,3456]{1,0:T(2,128)} %param.8) | copy-start | bytes 82948
